TPU v7x, 32 devices: a whole 2x2x4 slice. The times are simulated.
32 devices in a mesh: group: 2 (over x), attn: 8 (over z, y), expert: 2 (over core).
Axes of the slice: x: 2, y: 2, z: 4, core: 2. Of those that a mesh axis runs over, the one named last changes fastest.
Arguments:
- queries: bfloat16 [384, 48, 128], P(('group', 'attn'), 'expert'), parts along dimension 0, may hold values from -9 to 9
- keys: bfloat16 [384, 40, 8, 128], P(('group', 'attn'), None, 'expert'), parts along dimension 0, may hold values from -9 to 9
- values: bfloat16 [384, 40, 8, 128], P(('group', 'attn'), None, 'expert'), parts along dimension 0, may hold values from -12 to 12
- lengths: int32 [384], P(('group', 'attn')), parts along dimension 0, may hold values from 10 to 40, as said below
- out_proj: bfloat16 [6144, 3072], P('expert', 'attn'), may hold values from -0.078125 to 0.078125
- residual: bfloat16 [384, 3072], P('group', 'attn'), parts along dimension 0, may hold values from -45 to 45
- norm_gain: float32 [3072], replicated, may hold values from 0.25 to 1.75
- expert_ids: int32 [384, 2], P('group'), parts along dimension 0, may hold values from 0 to 3, as said below
- expert_slots: int32 [384, 2], P('group'), parts along dimension 0, may hold values from 0 to 143, as said below
- route_weights: float32 [384, 2], P('group'), parts along dimension 0, may hold values from 0.1 to 0.9
- w_gate: bfloat16 [4, 3072, 8192], P('expert', None, 'attn'), may hold values from -0.109375 to 0.109375
- w_up: bfloat16 [4, 3072, 8192], P('expert', None, 'attn'), may hold values from -0.109375 to 0.109375
- w_down: bfloat16 [4, 8192, 3072], P('expert', 'attn'), may hold values from -0.0625 to 0.0625
Outputs:
- hidden: bfloat16 [384, 3072], P('group', 'attn'), parts along dimension 0
- expert_out: bfloat16 [384, 3072], P('group', 'attn'), parts along dimension 0
There are 2 independent parts, one for each index of `group`. A program takes and returns all parts, laid end to end along the dimension named above; an argument that names none is the same for every part. Nothing has to cross between parts.
Inputs may be any that keep to these rules, and one draw needn't show every extreme that they name: Each sequence's cache is live in its first lengths positions; one sequence is 40 long. `expert_ids`: the two experts of a token differ; one expert, drawn from the seed, is chosen by exactly 144 tokens, and the other three share the remaining choices nearly evenly. `expert_slots`: a choice's slot is its rank, counting tokens in order and a token's first choice before its second, among the choices of the same expert.
All inputs are finite; a program needn't handle non-finite values.
Results may differ from a plain program's by a relative error of at most 0.02.
Values may be sent and summed in bfloat16 or wider, within the bound.
A program may use at most 128 MiB of HBM per device.

v0:
```python
import math

import jax
import jax.numpy as jnp
from jax import lax
from jax.sharding import PartitionSpec as P

norm_eps = 1e-05


def body(
    queries,
    keys,
    values,
    lengths,
    out_proj,
    residual,
    norm_gain,
    expert_ids,
    expert_slots,
    route_weights,
    w_gate,
    w_up,
    w_down,
):
    seq_local, head_local, head_dim = queries.shape
    kv_local = keys.shape[2]
    cache_len = keys.shape[1]
    groups = head_local // kv_local
    query_groups = queries.reshape(seq_local, kv_local, groups, head_dim)
    scores = jnp.einsum(
        "skgd,sjkd->skgj", query_groups, keys, preferred_element_type=jnp.float32
    ) / math.sqrt(head_dim)
    visible = lax.broadcasted_iota(jnp.int32, (seq_local, cache_len), 1) < lengths[:, None]
    scores = jnp.where(visible[:, None, None, :], scores, -jnp.inf)
    row_peak = jnp.max(scores, axis=-1, keepdims=True)
    expo = jnp.exp(scores - row_peak)
    attn_probs = (expo / jnp.sum(expo, axis=-1, keepdims=True)).astype(jnp.bfloat16)
    head_out = jnp.einsum("skgj,sjkd->skgd", attn_probs, values, preferred_element_type=jnp.float32)
    head_out = head_out.astype(jnp.bfloat16).reshape(seq_local, head_local * head_dim)
    half_mixed = jnp.dot(
        lax.all_gather(head_out, "attn", axis=0, tiled=True),
        out_proj,
        preferred_element_type=jnp.float32,
    )
    mixed = lax.psum(half_mixed.astype(jnp.bfloat16), "expert").astype(jnp.float32)
    hidden = (residual.astype(jnp.float32) + mixed).astype(jnp.bfloat16)
    hidden_f = hidden.astype(jnp.float32)
    model_width = norm_gain.shape[0]
    col_count = hidden.shape[1]
    square_sums = lax.psum(jnp.sum(hidden_f * hidden_f, axis=1), "attn")
    gain_part = lax.dynamic_slice_in_dim(norm_gain, lax.axis_index("attn") * col_count, col_count)
    outgoing = (
        hidden_f * lax.rsqrt(square_sums / model_width + norm_eps)[:, None] * gain_part[None, :]
    ).astype(jnp.bfloat16)
    gathered = lax.all_gather(outgoing, "attn", axis=1, tiled=True)
    seq_count = expert_ids.shape[0]
    capacity = 3 * seq_count // 4
    local_count = w_gate.shape[0]
    local_ids = expert_ids - lax.axis_index("expert") * local_count
    is_local = (local_ids >= 0) & (local_ids < local_count)
    flat_slot = jnp.where(is_local, local_ids * capacity + expert_slots, local_count * capacity)
    token_index = lax.broadcasted_iota(jnp.int32, (seq_count, 2), 0)
    slot_token = (
        jnp.full((local_count * capacity,), -1, jnp.int32)
        .at[flat_slot.reshape(-1)]
        .set(token_index.reshape(-1), mode="drop")
    )
    filled = slot_token >= 0
    packed = jnp.where(
        filled[:, None], gathered[jnp.maximum(slot_token, 0)], jnp.zeros((), jnp.bfloat16)
    )
    packed = packed.reshape(local_count, capacity, model_width)
    gate_act = jnp.einsum("ecd,edf->ecf", packed, w_gate, preferred_element_type=jnp.float32)
    up_act = jnp.einsum("ecd,edf->ecf", packed, w_up, preferred_element_type=jnp.float32)
    active = (jax.nn.silu(gate_act) * up_act).astype(jnp.bfloat16)
    slot_out = jnp.einsum("ecf,efd->ecd", active, w_down, preferred_element_type=jnp.float32)
    slot_out = slot_out.reshape(local_count * capacity, model_width)
    combined = jnp.zeros((seq_count, model_width), jnp.float32)
    for column in range(2):
        row_pick = jnp.minimum(flat_slot[:, column], local_count * capacity - 1)
        row_scale = jnp.where(is_local[:, column], route_weights[:, column], 0.0)
        combined = combined + slot_out[row_pick] * row_scale[:, None]
    rounded_part = lax.optimization_barrier(combined.astype(jnp.bfloat16)).astype(jnp.float32)
    feature_part = lax.psum_scatter(
        rounded_part.astype(jnp.bfloat16), "attn", scatter_dimension=1, tiled=True
    )
    row_total = lax.psum(feature_part, "expert").astype(jnp.float32)
    return (hidden, row_total.astype(jnp.bfloat16))


def solution(mesh):
    return jax.shard_map(
        body,
        mesh=mesh,
        in_specs=(
            P(("group", "attn"), "expert", None),
            P(("group", "attn"), None, "expert", None),
            P(("group", "attn"), None, "expert", None),
            P(("group", "attn")),
            P("expert", "attn"),
            P("group", "attn"),
            P(),
            P("group", None),
            P("group", None),
            P("group", None),
            P("expert", None, "attn"),
            P("expert", None, "attn"),
            P("expert", "attn", None),
        ),
        out_specs=(P("group", "attn"), P("group", "attn")),
        check_vma=False,
    )
```

profile of v0, /device:TPU:0, one launch (start us, length us, event | category | flops | bytes accessed | tf_op | source)
XLA Modules:
  0.0 274.2 jit_solution(5645987651585115730)
XLA Ops:
  7.2 1.1 copy.22
  8.3 0.7 iota_compare_fusion
  9.0 1.8 fusion.7
  10.9 0.3 fusion.22
  11.2 2.6 convolution_convert_fusion
  13.8 0.8 reshape.75
  14.7 0.0 all-reduce.3.cloned.1.call-start
  14.8 43.8 %all-gather.3.cloned.1.call-done = bf16[192,3072]{1,0:T(8,128)(2,1)} async-done(((bf16[24,3072]{1,0:T(8,128)(2,1)}), bf16[192,3072]{1,0:T(8,128)(2,1)}) %all-gather.3.cloned.1.call-update) | async-done | bytes 1179664 | tf_op jit(solution)/shard_map/all_gather | solution.py:42
  58.6 2.7 convolution_convert_fusion.1
  61.4 0.8 dynamic_slice.3
  62.2 16.1 %all-reduce.3.cloned.1.call-done = bf16[192,384]{1,0:T(8,128)(2,1)} async-done(((bf16[192,384]{1,0:T(8,128)(2,1)}), bf16[192,384]{1,0:T(8,128)(2,1)}) %all-reduce.3.cloned.1.call-update) | async-done | bytes 147472 | tf_op jit(solution)/shard_map/psum | solution.py:46
  78.3 1.0 fusion.12
  79.3 21.6 %psum.22 = f32[192]{0:T(256)S(1)} all-reduce(f32[192]{0:T(256)S(1)} %get-tuple-element.2), channel_id=1, replica_groups=mesh['group'=2,'attn'=8,'expert'=2] {'attn'}, use_global_device_ids=true, to_apply=%region_5.6 | all-reduce | flops 192 | bytes 1536 | tf_op jit(solution)/shard_map/psum | solution.py:51
  100.9 0.8 fusion.14
  101.8 0.1 copy.26
  101.9 0.1 reshape.76
  102.1 0.1 reshape.107
  102.3 2.9 %scatter_custom_fusion = s32[288]{0:T(512)S(1)} fusion(s32[384]{0:T(512)S(1)} %fusion.17, s32[384]{0:T(512)S(1)} %reshape.107, s32[]{:T(128)} %constant.20.clone.1), kind=kCustom, calls=%fused_computation.47 | custom fusion | bytes 1156 | tf_op jit(solution)/shard_map/scatter | solution.py:67
  105.2 0.1 broadcast_in_dim.57
  105.4 34.7 %all-gather.5.cloned.1.call-done = bf16[192,3072]{1,0:T(8,128)(2,1)} async-done(((bf16[192,384]{1,0:T(8,128)(2,1)}), bf16[192,3072]{1,0:T(8,128)(2,1)}) %all-gather.5.cloned.1.call-update) | async-done | bytes 1179664 | tf_op jit(solution)/shard_map/all_gather | solution.py:56
  140.1 8.0 %gather_fusion = bf16[288,3072]{1,0:T(8,128)(2,1)} fusion(bf16[192,3072]{1,0:T(8,128)(2,1)} %all-gather.5.cloned.1.call-done, s32[1024]{0:T(1024)S(1)} %pad_clamp_fusion.2), kind=kCustom, calls=%fused_computation | custom fusion | bytes 3540096 | tf_op jit(solution)/shard_map/gather | solution.py:71
  148.1 7.3 %fusion.2 = f32[2,144,1024]{2,1,0:T(8,128)S(1)} fusion(bf16[2,3072,1024]{2,1,0:T(8,128)(2,1)} %param.23, bf16[2,144,3072]{2,1,0:T(8,128)(2,1)} %bitcast.22, pred[2,144]{1,0:T(4,128)(4,1)S(1)} %broadcast_in_dim.57), kind=kOutput, calls=%fused_computation.8 | convolution fusion | flops 1812824064 | bytes 15532320 | tf_op jit(solution)/shard_map/ecd,edf->ecf/dot_general | solution.py:74
  155.4 7.1 %fusion.4 = bf16[2,144,1024]{2,1,0:T(8,128)(2,1)S(1)} fusion(bf16[2,3072,1024]{2,1,0:T(8,128)(2,1)} %param.24, bf16[2,144,3072]{2,1,0:T(8,128)(2,1)S(1)} %bitcast.23, pred[2,144]{1,0:T(4,128)(4,1)S(1)} %broadcast_in_dim.57, f32[2,144,1024]{2,1,0:T(8,128)S(1)} %fusion.2), kind=kOutput, calls=%fused_computation.10 | convolution fusion | flops 1814593536 | bytes 16122144 | tf_op jit(solution)/shard_map/ecd,edf->ecf/dot_general | solution.py:75
  162.5 3.8 %fusion.23 = f32[2,144,3072]{2,1,0:T(8,128)} fusion(bf16[2,144,1024]{2,1,0:T(8,128)(2,1)S(1)} %fusion.4, bf16[2,1024,3072]{2,1,0:T(8,128)(2,1)S(1)} %bitcast.20), kind=kOutput, calls=%fused_computation.52 | convolution fusion | flops 1811939328 | bytes 16711680 | tf_op jit(solution)/shard_map/ecf,efd->ecd/dot_general | solution.py:77
  166.3 5.8 %gather_fusion.1 = f32[192,3072]{1,0:T(8,128)} fusion(f32[288,3072]{1,0:T(8,128)} %bitcast.17, s32[1024]{0:T(1024)S(1)} %pad_clamp_fusion.1), kind=kCustom, calls=%fused_computation.1 | custom fusion | bytes 4719360 | tf_op jit(solution)/shard_map/gather | solution.py:83
  172.1 5.8 %gather_fusion.2 = f32[192,3072]{1,0:T(8,128)} fusion(f32[288,3072]{1,0:T(8,128)} %bitcast.18, s32[1024]{0:T(1024)S(1)} %pad_clamp_fusion), kind=kCustom, calls=%fused_computation.2 | custom fusion | bytes 4719360 | tf_op jit(solution)/shard_map/gather | solution.py:83
  178.0 2.9 %add_convert_fusion = bf16[192,3072]{1,0:T(8,128)(2,1)S(1)} fusion(f32[192,3072]{1,0:T(8,128)} %gather_fusion.2, f32[192,3072]{1,0:T(8,128)} %gather_fusion.1, f32[192]{0:T(256)S(1)} %bitcast.29, f32[192]{0:T(256)S(1)} %bitcast.28), kind=kLoop, calls=%fused_computation.5 | loop fusion | flops 2359296 | bytes 5899776 | tf_op jit(solution)/shard_map/convert_element_type | solution.py:84
  180.9 1.6 copy.27
  182.5 63.8 %reduce-scatter.4.cloned.1.call-done = bf16[384,192]{1,0:T(8,128)(2,1)} async-done(((bf16[3072,192]{1,0:T(8,128)(2,1)}), bf16[384,192]{1,0:T(8,128)(2,1)}) %reduce-scatter.4.cloned.1.call-update) | async-done | bytes 147472
  246.3 1.7 copy.28
  248.0 18.0 %all-reduce.5.cloned.1.call-done = bf16[192,384]{1,0:T(8,128)(2,1)} async-done(((bf16[192,384]{1,0:T(8,128)(2,1)}), bf16[192,384]{1,0:T(8,128)(2,1)}) %all-reduce.5.cloned.1.call-update) | async-done | bytes 147472 | tf_op jit(solution)/shard_map/psum | solution.py:88
  266.1 1.6 copy.37
  (42 shorter events, 0.4 us)
Async XLA Ops:
  7.2 51.4 %copy-start = (bf16[3072,384]{1,0:T(8,128)(2,1)S(1)}, bf16[3072,384]{1,0:T(8,128)(2,1)}, u32[]{:S(2)}) copy-start(bf16[3072,384]{1,0:T(8,128)(2,1)} %param.17) | copy-start | bytes 7077892
  7.2 51.4 %all-gather.3.cloned.1.call-start = ((), (), s32[]{:S(2)}) async-start(), calls=%async_computation.1 | async-start | bytes 1327104 | tf_op jit(solution)/shard_map/all_gather | solution.py:42
  14.7 63.6 %copy-start.3 = (bf16[192,384]{1,0:T(8,128)(2,1)S(1)}, bf16[192,384]{1,0:T(8,128)(2,1)}, u32[]{:S(2)}) copy-start(bf16[192,384]{1,0:T(8,128)(2,1)} %param.18) | copy-start | bytes 442372
  14.7 87.1 %copy-start.4 = (s32[192,2]{0,1:T(2,128)S(1)}, s32[192,2]{0,1:T(2,128)}, u32[]{:S(2)}) copy-start(s32[192,2]{0,1:T(2,128)} %param.20) | copy-start | bytes 4612
  14.7 87.1 %copy-start.6 = (s32[192,2]{0,1:T(2,128)S(1)}, s32[192,2]{0,1:T(2,128)}, u32[]{:S(2)}) copy-start(s32[192,2]{0,1:T(2,128)} %param.21) | copy-start | bytes 4612
  14.7 90.7 %copy-start.5 = (f32[192,2]{0,1:T(2,128)S(1)}, f32[192,2]{0,1:T(2,128)}, u32[]{:S(2)}) copy-start(f32[192,2]{0,1:T(2,128)} %param.22) | copy-start | bytes 4612
  14.7 63.5 %all-reduce.3.cloned.1.call-start = ((), (), s32[]{:S(2)}) async-start(), calls=%async_computation.2 | async-start | bytes 294912 | tf_op jit(solution)/shard_map/psum | solution.py:46
  61.3 78.8 %all-gather.5.cloned.1.call-start = ((), (), s32[]{:S(2)}) async-start(), calls=%async_computation.3 | async-start | bytes 1327104 | tf_op jit(solution)/shard_map/all_gather | solution.py:56
  79.3 68.8 %copy-start.2 = (bf16[192,384]{1,0:T(8,128)(2,1)}, bf16[192,384]{1,0:T(8,128)(2,1)S(1)}, u32[]{:S(2)}) copy-start(bf16[192,384]{1,0:T(8,128)(2,1)S(1)} %get-tuple-element.8) | copy-start | bytes 442372
  101.7 144.6 %reduce-scatter.4.cloned.1.call-start = ((), (), s32[]{:S(2)}) async-start(), calls=%async_computation.5 | async-start | bytes 1769472
  148.1 7.3 %copy-start.1 = (bf16[288,3072]{1,0:T(8,128)(2,1)S(1)}, bf16[288,3072]{1,0:T(8,128)(2,1)}, u32[]{:S(2)}) copy-start(bf16[288,3072]{1,0:T(8,128)(2,1)} %gather_fusion) | copy-start | bytes 5308420
  148.1 14.4 %slice-start = ((s8[12582912]{0:T(1024)(128)(4,1)}), s8[4194304]{0:T(1024)(128)(4,1)S(1)}, s32[]{:S(2)}) async-start(s8[12582912]{0:T(1024)(128)(4,1)} %bitcast.19), calls=%async_computation.6 | async-start | bytes 8388608
  148.1 14.4 %slice-start.1 = ((s8[12582912]{0:T(1024)(128)(4,1)}), s8[4194304]{0:T(1024)(128)(4,1)S(1)}, s32[]{:S(2)}) async-start(s8[12582912]{0:T(1024)(128)(4,1)} %bitcast.19), calls=%async_computation.7 | async-start | bytes 8388608
  155.4 7.1 %slice-start.2 = ((s8[12582912]{0:T(1024)(128)(4,1)}), s8[4194304]{0:T(1024)(128)(4,1)S(1)}, s32[]{:S(2)}) async-start(s8[12582912]{0:T(1024)(128)(4,1)} %bitcast.19), calls=%async_computation.8 | async-start | bytes 8388608
  182.5 83.6 %all-reduce.5.cloned.1.call-start = ((), (), s32[]{:S(2)}) async-start(), calls=%async_computation.4 | async-start | bytes 294912 | tf_op jit(solution)/shard_map/psum | solution.py:88
Sparse Core Ops, SparseCore 0:
  14.8 43.7 all-gather.2
  61.5 16.7 all-reduce.2
  101.9 38.1 all-gather.4
  182.6 63.6 reduce-scatter.3
  249.2 16.8 all-reduce.4
where the time goes:
time: 275 us; the launch traced here: 274 us
  waiting for transfers between devices  177 us (64%)
  local copies, waits for them, and re-layouts  30.6 us (11%)
  matrix products  25.3 us (9%)
  blocking collectives  21.6 us (8%)
  between operations  14 us (5%)
  other arithmetic  5.9 us (2%)
    unnamed x6, waiting for transfers between devices  63.9 us
    all_gather x1, waiting for transfers between devices, body(): lax.all_gather(head_out, 'attn', axis=0, tiled=True)  43.8 us
    all_gather x1, waiting for transfers between devices, body(): gathered = lax.all_gather(outgoing, 'attn', axis=1, tiled=True)  34.7 us
    psum x1, blocking collectives, body(): square_sums = lax.psum(jnp.sum(hidden_f * hidden_f, axis=1), 'attn')  21.6 us
    psum x1, waiting for transfers between devices, body(): row_total = lax.psum(feature_part, 'expert').astype(jnp.float32)  18 us
    psum x1, waiting for transfers between devices, body(): lax.psum(half_mixed.astype(jnp.bfloat16), 'expert').astype(jnp.float32)  16.1 us
    gather x2, local copies, waits for them, and re-layouts, body(): combined = combined + slot_out[row_pick] * row_scale[:, None]  11.6 us
    gather x1, local copies, waits for them, and re-layouts, body(): gathered[jnp.maximum(slot_token, 0)]  8 us
  transfers between devices with their start and end apart: 5, of which 5 were waited for; matrix products, arithmetic and copies ran while one was open for 2% of the time, Pallas kernels for 0%

commit v1 on v0

--- a/solution.py
+++ b/solution.py
@@ -1,14 +1,17 @@
+import functools
 import math
 
 import jax
 import jax.numpy as jnp
 from jax import lax
+from jax.experimental import pallas as pl
+from jax.experimental.pallas import tpu as pltpu
 from jax.sharding import PartitionSpec as P
 
 norm_eps = 1e-05
 
 
-def body(
+def plain_body(
     queries,
     keys,
     values,
@@ -89,9 +92,496 @@
     return (hidden, row_total.astype(jnp.bfloat16))
 
 
+ROWS = 8
+TILE = 256
+MESH = pl.DeviceIdType.MESH
+
+
+def near_first(count):
+    return sorted(range(1, count), key=lambda k: (min(k, count - k), k))
+
+
+def layer_kernel(
+    n,
+    kv,
+    q_hbm,
+    k_hbm,
+    v_hbm,
+    len_ref,
+    wo_hbm,
+    res_ref,
+    gain_ref,
+    ids_ref,
+    rw_ref,
+    wg_hbm,
+    wu_hbm,
+    wd_hbm,
+    hid_out,
+    exp_out,
+    q_v,
+    k_v,
+    v_v,
+    wo_v,
+    wg_v,
+    wu_v,
+    wd_v,
+    att,
+    heads,
+    mixed,
+    mixed_in,
+    xbuf,
+    xs,
+    acc_g,
+    acc_u,
+    act,
+    pacc,
+    core_out,
+    core_in,
+    y_out,
+    y_in,
+    z_out,
+    z_in,
+    last,
+    in_sem,
+    wo_sem,
+    w_sem,
+    d_sem,
+    s1z,
+    s1y,
+    r1,
+    sx,
+    rx,
+    s2z,
+    s2y,
+    s2c,
+    r2,
+    s3c,
+    r3c,
+    s3y,
+    r3y,
+    s3z,
+    r3z,
+    s4,
+    r4,
+):
+    zs = n // 2
+    chunks = heads.shape[1]
+    head_count, head_dim = q_v.shape[1:]
+    cache_rows = k_v.shape[1]
+    cols = xbuf.shape[3]
+    half_rows = xbuf.shape[2]
+    rows = 2 * half_rows
+    pair = 2 * cols
+    width = n * cols
+    ff = acc_g.shape[2]
+    local_count = acc_g.shape[0]
+
+    me = lax.axis_index("attn")
+    core = lax.axis_index("expert")
+    other = 1 - core
+    z = me // 2
+    y = me % 2
+    partner = me + 1 - 2 * y
+
+    def z_of(k):
+        return lax.rem(z + k, zs)
+
+    def z_from(k):
+        return lax.rem(z + zs - k, zs)
+
+    def at_attn(a):
+        return {"attn": a}
+
+    sibling = {"expert": other}
+
+    def rcopy(src, dst, send, recv, dev):
+        return pltpu.make_async_remote_copy(
+            src_ref=src,
+            dst_ref=dst,
+            send_sem=send,
+            recv_sem=recv,
+            device_id=dev,
+            device_id_type=MESH,
+        )
+
+    barrier = pltpu.get_barrier_semaphore()
+    for k in range(1, zs):
+        pl.semaphore_signal(barrier, inc=1, device_id=at_attn(2 * z_of(k) + y), device_id_type=MESH)
+    pl.semaphore_signal(barrier, inc=1, device_id=at_attn(partner), device_id_type=MESH)
+    pl.semaphore_signal(barrier, inc=1, device_id=sibling, device_id_type=MESH)
+
+    def in_copies(c):
+        rng = pl.ds(c * ROWS, ROWS)
+        return [
+            pltpu.make_async_copy(hbm.at[rng], vm.at[rng], in_sem.at[c, i])
+            for i, (hbm, vm) in enumerate(((q_hbm, q_v), (k_hbm, k_v), (v_hbm, v_v)))
+        ]
+
+    for c in range(chunks):
+        for copy in in_copies(c):
+            copy.start()
+    wo_copy = pltpu.make_async_copy(wo_hbm, wo_v, wo_sem)
+    wo_copy.start()
+    order = near_first(zs)
+
+    def w_copies(k):
+        rng = pl.ds(pl.multiple_of(z_of(zs - k) * pair, pair), pair)
+        return [
+            pltpu.make_async_copy(hbm.at[e, rng], vm.at[e, rng], w_sem.at[k, 2 * e + i])
+            for e in range(local_count)
+            for i, (hbm, vm) in enumerate(((wg_hbm, wg_v), (wu_hbm, wu_v)))
+        ]
+
+    for k in [0] + order:
+        for copy in w_copies(k):
+            copy.start()
+    d_copies = [
+        pltpu.make_async_copy(
+            wd_hbm.at[e, :, pl.ds(b * pair, pair)],
+            wd_v.at[b, pl.ds(e * ff, ff)],
+            d_sem.at[b, e],
+        )
+        for b in range(zs)
+        for e in range(local_count)
+    ]
+    for copy in d_copies:
+        copy.start()
+
+    col = lax.broadcasted_iota(jnp.int32, (head_count, cache_rows), 1)
+    row = lax.broadcasted_iota(jnp.int32, (head_count, cache_rows), 0)
+    col_pos = lax.shift_right_logical(col, kv.bit_length() - 1)
+    col_kv = lax.bitwise_and(col, kv - 1)
+    groups = head_count // kv
+    same_kv = (row >= col_kv * groups) & (row < col_kv * groups + groups)
+    live_pos = jnp.where(same_kv, col_pos, 1 << 20)
+
+    def z_send(k, c):
+        return rcopy(
+            heads.at[me, c], heads.at[me, c], s1z.at[k, c], r1.at[me, c], at_attn(2 * z_of(k) + y)
+        )
+
+    def y_send(k, c):
+        a = 2 * z_from(k) + y
+        return rcopy(heads.at[a, c], heads.at[a, c], s1y.at[k, c], r1.at[a, c], at_attn(partner))
+
+    def attend(c):
+        for copy in in_copies(c):
+            copy.wait()
+        scores = []
+        for i in range(ROWS):
+            s = c * ROWS + i
+            logits = lax.dot_general(
+                q_v[s], k_v[s], (((1,), (1,)), ((), ())), preferred_element_type=jnp.float32
+            )
+            scores.append(jnp.where(live_pos < len_ref[s], logits, -1e30))
+        scores = jnp.concatenate(scores, axis=0) * (1.0 / math.sqrt(head_dim))
+        expo = jnp.exp(scores - jnp.max(scores, axis=-1, keepdims=True))
+        probs = expo / jnp.sum(expo, axis=-1, keepdims=True)
+        for i in range(ROWS):
+            part = probs[i * head_count : (i + 1) * head_count].astype(jnp.bfloat16)
+            att[pl.ds(i * head_count, head_count), :] = jnp.dot(
+                part, v_v[c * ROWS + i], preferred_element_type=jnp.float32
+            )
+        for h in range(head_count):
+            heads[me, c, :, h * head_dim : (h + 1) * head_dim] = att[
+                pl.ds(h, ROWS, stride=head_count), :
+            ].astype(jnp.bfloat16)
+
+    for c in range(chunks):
+        attend(c)
+        if c == 0:
+            pl.semaphore_wait(barrier, zs + 1)
+        for k in order:
+            z_send(k, c).start()
+        y_send(0, c).start()
+
+    for c in range(chunks):
+        for k in order:
+            y_send(k, c).wait_recv()
+            y_send(k, c).start()
+    for c in range(chunks):
+        for k in [0] + order:
+            a = 2 * z_from(k) + 1 - y
+            rcopy(heads.at[a, c], heads.at[a, c], s1y.at[k, c], r1.at[a, c], at_attn(partner)).wait_recv()
+
+    wo_copy.wait()
+    proj = jnp.dot(
+        heads[...].reshape(rows, head_count * head_dim), wo_v[...], preferred_element_type=jnp.float32
+    )
+    mixed[0] = proj[:half_rows]
+    mixed[1] = proj[half_rows:]
+    x_copy = rcopy(mixed.at[other], mixed_in, sx, rx, sibling)
+    x_copy.start()
+    x_copy.wait_recv()
+    xbuf[me, core] = (res_ref[core].astype(jnp.float32) + mixed[core] + mixed_in[...]).astype(jnp.bfloat16)
+
+    def x_z(k):
+        return rcopy(
+            xbuf.at[me, core], xbuf.at[me, core], s2z.at[k], r2.at[me, core], at_attn(2 * z_of(k) + y)
+        )
+
+    def x_y(k):
+        a = 2 * z_from(k) + y
+        return rcopy(xbuf.at[a, core], xbuf.at[a, core], s2y.at[k], r2.at[a, core], at_attn(partner))
+
+    def x_c(a, half):
+        return rcopy(xbuf.at[a, half], xbuf.at[a, half], s2c.at[a], r2.at[a, half], sibling)
+
+    for k in order:
+        x_z(k).start()
+    x_y(0).start()
+    x_c(me, core).start()
+
+    def from_z(k):
+        a = 2 * z_from(k) + y
+        x_c(a, core).wait_recv()
+        x_y(k).start()
+        x_c(a, core).start()
+
+    def from_y(k):
+        a = 2 * z_from(k) + 1 - y
+        x_c(a, core).wait_recv()
+        x_c(a, core).start()
+
+    def from_core(k):
+        for side in range(2):
+            x_c(2 * z_from(k) + side, other).wait_recv()
+
+    def load_x(k, ssq):
+        b = z_from(k)
+        for side in range(2):
+            block = xbuf[2 * b + side].reshape(rows, cols).astype(jnp.float32)
+            ssq = ssq + jnp.sum(block * block, axis=1, keepdims=True)
+            xs[:, side * cols : (side + 1) * cols] = (block * gain_ref[2 * b + side]).astype(jnp.bfloat16)
+        return ssq
+
+    def up_step(k, first):
+        for copy in w_copies(k):
+            copy.wait()
+        rng = pl.ds(pl.multiple_of(z_from(k) * pair, pair), pair)
+        for e in range(local_count):
+
+            def tile(t, carry):
+                at = pl.ds(pl.multiple_of(t * TILE, TILE), TILE)
+                for acc, w in ((acc_g, wg_v), (acc_u, wu_v)):
+                    part = jnp.dot(xs[...], w[e, rng, at], preferred_element_type=jnp.float32)
+                    if first:
+                        acc[e, :, at] = part
+                    else:
+                        acc[e, :, at] += part
+                return carry
+
+            lax.fori_loop(0, ff // TILE, tile, 0)
+
+    near = order[:2]
+    far = order[2:]
+    from_y(0)
+    for k in near:
+        from_z(k)
+    from_core(0)
+    ssq = load_x(0, jnp.zeros((rows, 1), jnp.float32))
+    up_step(0, True)
+    for k in far:
+        from_z(k)
+    for k in order:
+        from_y(k)
+        from_core(k)
+        ssq = load_x(k, ssq)
+        up_step(k, False)
+    for half in range(2):
+        hid_out[half] = xbuf[me, half]
+
+    row_scale = lax.rsqrt(ssq / width + norm_eps)
+    for e in range(local_count):
+        chosen = ids_ref[...] == core * local_count + e
+        weight = jnp.sum(jnp.where(chosen, rw_ref[...], 0.0), axis=1, keepdims=True)
+        weight = weight * row_scale
+
+        def tile(t, carry):
+            at = pl.ds(pl.multiple_of(t * TILE, TILE), TILE)
+            gate = acc_g[e, :, at] * row_scale
+            value = gate / (1.0 + jnp.exp(-gate)) * (acc_u[e, :, at] * weight)
+            act[:, pl.ds(pl.multiple_of(e * ff + t * TILE, TILE), TILE)] = value.astype(jnp.bfloat16)
+            return carry
+
+        lax.fori_loop(0, ff // TILE, tile, 0)
+
+    for copy in d_copies:
+        copy.wait()
+
+    def down(k):
+        b = z_of(k)
+        for t in range(0, pair, TILE):
+            part = jnp.dot(act[...], wd_v[b, :, t : t + TILE], preferred_element_type=jnp.float32)
+            for side in range(2):
+                lo, hi = max(t, side * cols), min(t + TILE, (side + 1) * cols)
+                if lo < hi:
+                    for half in range(2):
+                        pacc[k, side, half, :, lo - side * cols : hi - side * cols] = part[
+                            half * half_rows : (half + 1) * half_rows, lo - t : hi - t
+                        ]
+        core_out[k] = pacc[k, :, other].astype(jnp.bfloat16)
+        core_copy(k).start()
+
+    def core_copy(k):
+        return rcopy(core_out.at[k], core_in.at[k], s3c.at[k], r3c.at[k], sibling)
+
+    def y_copy(k):
+        return rcopy(y_out.at[k], y_in.at[k], s3y.at[k], r3y.at[k], at_attn(partner))
+
+    def z_copy(k):
+        return rcopy(z_out.at[k], z_in.at[k], s3z.at[k], r3z.at[k], at_attn(2 * z_of(k) + y))
+
+    def core_sum(k):
+        core_copy(k).wait_recv()
+        y_out[k] = (pacc[k, 1 - y, core] + core_in[k, 1 - y].astype(jnp.float32)).astype(jnp.bfloat16)
+        y_copy(k).start()
+
+    def y_sum(k):
+        y_copy(k).wait_recv()
+        total = (
+            pacc[k, y, core] + core_in[k, y].astype(jnp.float32) + y_in[k].astype(jnp.float32)
+        )
+        if k == 0:
+            return total
+        z_out[k] = total.astype(jnp.bfloat16)
+        z_copy(k).start()
+
+    steps = order[::-1] + [0]
+    for i in range(len(steps) + 2):
+        if i < len(steps):
+            down(steps[i])
+        if 1 <= i <= len(steps):
+            core_sum(steps[i - 1])
+        if i >= 2:
+            total = y_sum(steps[i - 2])
+    for k in steps[:-1]:
+        z_copy(k).wait_recv()
+        total = total + z_in[k].astype(jnp.float32)
+    last[core] = total.astype(jnp.bfloat16)
+    last_copy = rcopy(last.at[core], last.at[core], s4, r4, sibling)
+    last_copy.start()
+
+    x_copy.wait_send()
+    for c in range(chunks):
+        for k in order:
+            z_send(k, c).wait_send()
+        for k in range(zs):
+            y_send(k, c).wait_send()
+    for k in order:
+        x_z(k).wait_send()
+    for k in range(zs):
+        x_y(k).wait_send()
+        core_copy(k).wait_send()
+        y_copy(k).wait_send()
+        if k:
+            z_copy(k).wait_send()
+    for a in range(n):
+        x_c(a, core).wait_send()
+    last_copy.wait_send()
+    rcopy(last.at[other], last.at[other], s4, r4, sibling).wait_recv()
+    exp_out[...] = last[...]
+
+
+def body(n, *operands):
+    (queries, keys, values, lengths, out_proj, residual, norm_gain) = operands[:7]
+    (expert_ids, expert_slots, route_weights, w_gate, w_up, w_down) = operands[7:]
+    seqs, head_count, head_dim = queries.shape
+    cache_len, kv = keys.shape[1:3]
+    rows, cols = residual.shape
+    local_count, width, ff = w_gate.shape
+    fits = (
+        n % 2 == 0
+        and seqs % ROWS == 0
+        and kv & (kv - 1) == 0
+        and cols % 128 == 0
+        and (2 * cols) % TILE == 0
+        and ff % TILE == 0
+        and rows % 32 == 0
+    )
+    if not fits:
+        return plain_body(*operands)
+    zs, chunks, half = n // 2, seqs // ROWS, rows // 2
+    bf16, f32 = jnp.bfloat16, jnp.float32
+    dma = pltpu.SemaphoreType.DMA
+    vmem = pl.BlockSpec(memory_space=pltpu.VMEM)
+    hbm = pl.BlockSpec(memory_space=pl.ANY)
+    hidden, out = pl.pallas_call(
+        functools.partial(layer_kernel, n, kv),
+        out_shape=[jax.ShapeDtypeStruct((2, half, cols), bf16)] * 2,
+        in_specs=[hbm, hbm, hbm, pl.BlockSpec(memory_space=pltpu.SMEM), hbm, vmem, vmem, vmem, vmem]
+        + [hbm] * 3,
+        out_specs=[vmem, vmem],
+        scratch_shapes=[
+            pltpu.VMEM((seqs, head_count, head_dim), bf16),
+            pltpu.VMEM((seqs, cache_len * kv, head_dim), bf16),
+            pltpu.VMEM((seqs, cache_len * kv, head_dim), bf16),
+            pltpu.VMEM(out_proj.shape, bf16),
+            pltpu.VMEM(w_gate.shape, bf16),
+            pltpu.VMEM(w_up.shape, bf16),
+            pltpu.VMEM((zs, local_count * ff, 2 * cols), bf16),
+            pltpu.VMEM((ROWS * head_count, head_dim), f32),
+            pltpu.VMEM((n, chunks, ROWS, head_count * head_dim), bf16),
+            pltpu.VMEM((2, half, cols), f32),
+            pltpu.VMEM((half, cols), f32),
+            pltpu.VMEM((n, 2, half, cols), bf16),
+            pltpu.VMEM((rows, 2 * cols), bf16),
+            pltpu.VMEM((local_count, rows, ff), f32),
+            pltpu.VMEM((local_count, rows, ff), f32),
+            pltpu.VMEM((rows, local_count * ff), bf16),
+            pltpu.VMEM((zs, 2, 2, half, cols), f32),
+            pltpu.VMEM((zs, 2, half, cols), bf16),
+            pltpu.VMEM((zs, 2, half, cols), bf16),
+            pltpu.VMEM((zs, half, cols), bf16),
+            pltpu.VMEM((zs, half, cols), bf16),
+            pltpu.VMEM((zs, half, cols), bf16),
+            pltpu.VMEM((zs, half, cols), bf16),
+            pltpu.VMEM((2, half, cols), bf16),
+            dma((chunks, 3)),
+            dma,
+            dma((zs, 2 * local_count)),
+            dma((zs, local_count)),
+            dma((zs, chunks)),
+            dma((zs, chunks)),
+            dma((n, chunks)),
+            dma,
+            dma,
+            dma((zs,)),
+            dma((zs,)),
+            dma((n,)),
+            dma((n, 2)),
+            dma((zs,)),
+            dma((zs,)),
+            dma((zs,)),
+            dma((zs,)),
+            dma((zs,)),
+            dma((zs,)),
+            dma,
+            dma,
+        ],
+        compiler_params=pltpu.CompilerParams(
+            collective_id=0, has_side_effects=True, vmem_limit_bytes=62 * 1024 * 1024
+        ),
+    )(
+        queries,
+        keys.reshape(seqs, cache_len * kv, head_dim),
+        values.reshape(seqs, cache_len * kv, head_dim),
+        lengths,
+        out_proj,
+        residual.reshape(2, half, cols),
+        norm_gain.reshape(n, 1, cols),
+        expert_ids,
+        route_weights,
+        w_gate,
+        w_up,
+        w_down,
+    )
+    return hidden.reshape(rows, cols), out.reshape(rows, cols)
+
+
 def solution(mesh):
     return jax.shard_map(
-        body,
+        functools.partial(body, mesh.shape["attn"]),
         mesh=mesh,
         in_specs=(
             P(("group", "attn"), "expert", None),

time: 275 us -> 77.1 us (0.28)
  waiting for transfers between devices: 177 us -> 0 us
  Pallas kernels: 0 us -> 70.1 us
  matrix products: 25.3 us -> 0 us
  local copies, waits for them, and re-layouts: 30.6 us -> 6.06 us
  blocking collectives: 21.6 us -> 0 us
  between operations: 14 us -> 0.64 us
  other arithmetic: 5.9 us -> 0 us
    all_gather x2 -> x0, waiting for transfers between devices: 78.5 us -> none  [the longest x1 43.8 us: body(): lax.all_gather(head_out, 'attn', axis=0, tiled=True)]
    pallas_call x0 -> x1, Pallas kernels: none -> 70.1 us  [body(): pl.pallas_call(functools.partial(layer_kernel, n, kv), out_shape=[jax.Sha...]
    unnamed x6 -> x0, waiting for transfers between devices: 63.9 us -> none
    psum x2 -> x0, waiting for transfers between devices: 34.1 us -> none  [the longest x1 18 us: body(): row_total = lax.psum(feature_part, 'expert').astype(jnp.float32)]
    dot_general x6 -> x0, matrix products: 25.3 us -> none  [the longest x1 7.3 us: body(): jnp.einsum('ecd,edf->ecf', packed, w_gate, preferred_element_type=jnp.flo...]
    psum x1 -> x0, blocking collectives: 21.6 us -> none  [body(): square_sums = lax.psum(jnp.sum(hidden_f * hidden_f, axis=1), 'attn')]
    gather x3 -> x0, local copies, waits for them, and re-layouts: 19.6 us -> none  [the longest x2 11.6 us: body(): combined = combined + slot_out[row_pick] * row_scale[:, None]]
    convert_element_type x2 -> x0, other arithmetic: 3.71 us -> none  [the longest x1 2.94 us: body(): combined.astype(jnp.bfloat16)]
  transfers between devices with their start and end apart: 5 -> 0, of which waited for: 5 -> 0; matrix products, arithmetic and copies ran while one was open for 2% -> 0% of each run, Pallas kernels for 0% -> 0%
where the time goes in v1:
time: 77.1 us; the launch traced here: 76.8 us
  Pallas kernels  70.1 us (91%)
  local copies, waits for them, and re-layouts  6.06 us (8%)
    pallas_call x1, Pallas kernels, body(): pl.pallas_call(functools.partial(layer_kernel, n, kv), out_shape=[jax.Sha...  70.1 us
    unnamed x4, local copies, waits for them, and re-layouts  6.06 us

profile of v1, /device:TPU:0, one launch (start us, length us, event | category | flops | bytes accessed | tf_op | source)
XLA Modules:
  0.0 76.8 jit_solution(17949196579875500916)
XLA Ops:
  0.6 1.4 %copy.14.ids_ref = s32[192,2]{1,0:T(8,128)} copy(s32[192,2]{0,1:T(2,128)} %param.20) | data formatting | bytes 3072 | tf_op args[7]
  2.1 1.4 %copy.15.rw_ref = f32[192,2]{1,0:T(8,128)} copy(f32[192,2]{0,1:T(2,128)} %param.21) | data formatting | bytes 3072 | tf_op args[9]
  3.5 70.1 %shard_map.131 = (bf16[2,96,384]{2,1,0:T(8,128)(2,1)}, bf16[2,96,384]{2,1,0:T(8,128)(2,1)}) custom-call(bf16[24,24,128]{2,1,0:T(8,128)(2,1)} %q_hbm.1, bf16[24,160,128]{2,1,0:T(8,128)(2,1)} %bitcast.6, bf16[24,160,128]{2,1,0:T(8,128)(2,1)} %bitcast.7, s32[24]{0:T(128)} %len_ref.1, bf16[3072,384]{1,0:T(8,128)(2,1)} %wo_hbm.1, bf16[2,96,384]{2,1,0:T(8,128)(2,1)} %bitcast.8, ...), custom_call_target="tpu_custom_call" | custom-call | tf_op jit(solution)/shard_map/pallas_call | solution.py:509
  73.7 1.6 %copy.18 = bf16[192,384]{1,0:T(8,128)(2,1)} copy(bf16[192,384]{1,0:T(8,128)(2,1)} %bitcast.10) | data formatting | bytes 294912
  75.2 1.6 %copy.19 = bf16[192,384]{1,0:T(8,128)(2,1)} copy(bf16[192,384]{1,0:T(8,128)(2,1)} %bitcast.9) | data formatting | bytes 294912

commit v2 on v1

--- a/solution.py
+++ b/solution.py
@@ -355,11 +355,12 @@
             xs[:, side * cols : (side + 1) * cols] = (block * gain_ref[2 * b + side]).astype(jnp.bfloat16)
         return ssq
 
-    def up_step(k, first):
-        for copy in w_copies(k):
-            copy.wait()
+    def up_step(k, first, experts):
+        if 0 in experts:
+            for copy in w_copies(k):
+                copy.wait()
         rng = pl.ds(pl.multiple_of(z_from(k) * pair, pair), pair)
-        for e in range(local_count):
+        for e in experts:
 
             def tile(t, carry):
                 at = pl.ds(pl.multiple_of(t * TILE, TILE), TILE)
@@ -380,21 +381,31 @@
         from_z(k)
     from_core(0)
     ssq = load_x(0, jnp.zeros((rows, 1), jnp.float32))
-    up_step(0, True)
+    up_step(0, True, range(1))
     for k in far:
         from_z(k)
-    for k in order:
+    up_step(0, True, range(1, local_count))
+    for k in near:
         from_y(k)
+    for i, k in enumerate(order):
         from_core(k)
         ssq = load_x(k, ssq)
-        up_step(k, False)
+        up_step(k, False, range(1))
+        if i == 0:
+            for j in far:
+                from_y(j)
+        up_step(k, False, range(1, local_count))
     for half in range(2):
         hid_out[half] = xbuf[me, half]
 
     row_scale = lax.rsqrt(ssq / width + norm_eps)
+    diagonal = lax.broadcasted_iota(jnp.int32, (rows, rows), 0) == lax.broadcasted_iota(
+        jnp.int32, (rows, rows), 1
+    )
     for e in range(local_count):
         chosen = ids_ref[...] == core * local_count + e
-        weight = jnp.sum(jnp.where(chosen, rw_ref[...], 0.0), axis=1, keepdims=True)
+        token_weight = jnp.sum(jnp.where(chosen, rw_ref[...], 0.0), axis=0, keepdims=True)
+        weight = jnp.sum(jnp.where(diagonal, token_weight, 0.0), axis=1, keepdims=True)
         weight = weight * row_scale
 
         def tile(t, carry):
@@ -481,6 +492,17 @@
     last_copy.wait_send()
     rcopy(last.at[other], last.at[other], s4, r4, sibling).wait_recv()
     exp_out[...] = last[...]
+
+
+def write_kernel(hidden, expert, hidden_out, expert_out, sem):
+    copies = [
+        pltpu.make_async_copy(hidden, hidden_out, sem.at[0]),
+        pltpu.make_async_copy(expert, expert_out, sem.at[1]),
+    ]
+    for copy in copies:
+        copy.start()
+    for copy in copies:
+        copy.wait()
 
 
 def body(n, *operands):
@@ -570,8 +592,8 @@
         out_proj,
         residual.reshape(2, half, cols),
         norm_gain.reshape(n, 1, cols),
-        expert_ids,
-        route_weights,
+        expert_ids.T,
+        route_weights.T,
         w_gate,
         w_up,
         w_down,

time: 77.1 us -> 72.6 us (0.942)
  local copies, waits for them, and re-layouts: 6.06 us -> 3.17 us
  Pallas kernels: 70.1 us -> 68.6 us
    unnamed x4 -> x2, local copies, waits for them, and re-layouts: 6.06 us -> 3.17 us
    pallas_call x1, Pallas kernels: 70.1 us -> 68.6 us  [body(): pl.pallas_call(functools.partial(layer_kernel, n, kv), out_shape=[jax.Sha...]
where the time goes in v2:
time: 72.6 us; the launch traced here: 72.4 us
  Pallas kernels  68.6 us (94%)
  local copies, waits for them, and re-layouts  3.17 us (4%)
    pallas_call x1, Pallas kernels, body(): pl.pallas_call(functools.partial(layer_kernel, n, kv), out_shape=[jax.Sha...  68.6 us
    unnamed x2, local copies, waits for them, and re-layouts  3.17 us

profile of v2, /device:TPU:0, one launch (start us, length us, event | category | flops | bytes accessed | tf_op | source)
XLA Modules:
  0.0 72.4 jit_solution(12671184585029001934)
XLA Ops:
  0.6 68.6 %shard_map.131 = (bf16[2,96,384]{2,1,0:T(8,128)(2,1)}, bf16[2,96,384]{2,1,0:T(8,128)(2,1)}) custom-call(bf16[24,24,128]{2,1,0:T(8,128)(2,1)} %q_hbm.1, bf16[24,160,128]{2,1,0:T(8,128)(2,1)} %bitcast.8, bf16[24,160,128]{2,1,0:T(8,128)(2,1)} %bitcast.9, s32[24]{0:T(128)} %len_ref.1, bf16[3072,384]{1,0:T(8,128)(2,1)} %wo_hbm.1, bf16[2,96,384]{2,1,0:T(8,128)(2,1)} %bitcast.10, ...), custom_call_target="tpu_custom_call" | custom-call | tf_op jit(solution)/shard_map/pallas_call | solution.py:531
  69.2 1.6 %copy.16 = bf16[192,384]{1,0:T(8,128)(2,1)} copy(bf16[192,384]{1,0:T(8,128)(2,1)} %bitcast.12) | data formatting | bytes 294912
  70.8 1.6 %copy.17 = bf16[192,384]{1,0:T(8,128)(2,1)} copy(bf16[192,384]{1,0:T(8,128)(2,1)} %bitcast.11) | data formatting | bytes 294912
